TPU v7x, 32 devices: a whole 2x2x4 slice. The times are simulated.
32 devices in a mesh: batch: 4 (over x, core), ctx: 4 (over z), fsdp: 2 (over y).
Axes of the slice: x: 2, y: 2, z: 4, core: 2. Of those that a mesh axis runs over, the one named last changes fastest.
Arguments:
- layer_input: bfloat16 [8, 512, 1024], P(('batch', 'fsdp'), 'ctx'), may hold values from -6 to 6
- out_grad: bfloat16 [8, 512, 1024], P(('batch', 'fsdp'), 'ctx'), may hold values from -6 to 6
- span_order: int32 [4], replicated, may hold values from 0 to 3, each once
- inward: bfloat16 [1024, 3072], P('fsdp')
- inward_bias: bfloat16 [3072], P('fsdp'), may hold values from -3 to 3
- outward: bfloat16 [1024, 1024], P('fsdp'), may hold values from -1 to 1
- outward_bias: bfloat16 [1024], P('fsdp'), may hold values from -3 to 3
- expand: bfloat16 [1024, 4096], P('fsdp'), may hold values from -0.1875 to 0.1875
- expand_bias: bfloat16 [4096], P('fsdp'), may hold values from -3 to 3
- contract: bfloat16 [4096, 1024], P('fsdp'), may hold values from -0.09375 to 0.09375
- contract_bias: bfloat16 [1024], P('fsdp'), may hold values from -3 to 3
- first_gain: bfloat16 [1024], P('fsdp'), may hold values from 0.099609375 to 1.8984375
- first_bias: bfloat16 [1024], P('fsdp'), may hold values from -3 to 3
- second_gain: bfloat16 [1024], P('fsdp'), may hold values from 0.099609375 to 1.8984375
- second_bias: bfloat16 [1024], P('fsdp'), may hold values from -3 to 3
Outputs:
- output: bfloat16 [8, 512, 1024], P(('batch', 'fsdp'), 'ctx')
- input_grad: float32 [8, 512, 1024], P(('batch', 'fsdp'), 'ctx')
- inward_grad: float32 [1024, 3072], P('fsdp')
- inward_shift: float32 [3072], P('fsdp')
- outward_grad: float32 [1024, 1024], P('fsdp')
- outward_shift: float32 [1024], P('fsdp')
- expand_grad: float32 [1024, 4096], P('fsdp')
- expand_shift: float32 [4096], P('fsdp')
- contract_grad: float32 [4096, 1024], P('fsdp')
- contract_shift: float32 [1024], P('fsdp')
- first_scale: float32 [1024], P('fsdp')
- first_shift: float32 [1024], P('fsdp')
- second_scale: float32 [1024], P('fsdp')
- second_shift: float32 [1024], P('fsdp')
Inputs may be any that keep to these rules, and one draw needn't show every extreme that they name: `span_order`: each value appears once.
All inputs are finite; a program needn't handle non-finite values.
Results may differ from a plain program's by a relative error of at most 0.012.
The roundings to bfloat16 on the way count: a program that leaves them out, or rounds other values in their place, can miss the bound.
Values may be sent and summed in bfloat16 or wider, within the bound.
A program may use at most 320 MiB of HBM per device.

v0:
```python
import math

import jax
import jax.numpy as jnp
from jax import lax
from jax.sharding import PartitionSpec as P

HEAD_DIM = 64
ROT = 16


EPSILON = 1e-05
ROTARY_BASE = 10000.0
MASKED = -1e30
HALF_ROOT = 0.7071067811865476
NORMAL_PEAK = 0.3989422804014327


def norm_forward(values, factor, offset):
    center = values - jnp.mean(values, axis=-1, keepdims=True)
    inverse = lax.rsqrt(jnp.mean(center * center, axis=-1, keepdims=True) + EPSILON)
    normed = center * inverse
    return (normed * factor + offset, normed, inverse)


def norm_backward(upstream, normed, inverse, factor):
    scaled = upstream * factor
    middle = jnp.mean(scaled, axis=-1, keepdims=True)
    coupled = jnp.mean(scaled * normed, axis=-1, keepdims=True)
    result = inverse * (scaled - middle - normed * coupled)
    return (result, jnp.sum(upstream * normed, axis=0), jnp.sum(upstream, axis=0))


def gelu_value(before):
    return 0.5 * before * (1.0 + lax.erf(before * HALF_ROOT))


def gelu_slope(before):
    return (
        0.5 * (1.0 + lax.erf(before * HALF_ROOT))
        + before * jnp.exp(-0.5 * before * before) * NORMAL_PEAK
    )


def slot_positions(span_order, first_slot, slot_count, span_size):
    slot_index = first_slot + jnp.arange(slot_count, dtype=jnp.int32)
    owners = slot_index // (2 * span_size)
    places = jnp.arange(span_order.shape[0], dtype=jnp.int32)
    leading = jnp.sum(jnp.where(owners[:, None] == places[None, :], span_order[None, :], 0), axis=1)
    spans = 2 * span_order.shape[0]
    picked = jnp.where(slot_index // span_size % 2 == 0, leading, spans - 1 - leading)
    return picked * span_size + slot_index % span_size


def rotary_tables(positions):
    half_rot = ROT // 2
    angular = jnp.exp(
        jnp.arange(half_rot, dtype=jnp.float32) * (-2.0 * math.log(ROTARY_BASE) / ROT)
    )
    angles = positions.astype(jnp.float32)[:, None] * angular[None, :]
    angles = jnp.concatenate([angles, angles], axis=1)
    return (jnp.cos(angles), jnp.sin(angles))


def rotate(tensor, cosine, sine_table):
    half_rot = ROT // 2
    leading_part = tensor[..., :ROT]
    turned = jnp.concatenate([-leading_part[..., half_rot:], leading_part[..., :half_rot]], axis=-1)
    rotated = leading_part * cosine[:, None, :] + turned * sine_table[:, None, :]
    return jnp.concatenate([rotated, tensor[..., ROT:]], axis=-1)


def unrotate(tensor, cosine, sine_table):
    half_rot = ROT // 2
    leading_part = tensor[..., :ROT]
    weighted = leading_part * sine_table[:, None, :]
    turned = jnp.concatenate([weighted[..., half_rot:], -weighted[..., :half_rot]], axis=-1)
    return jnp.concatenate([leading_part * cosine[:, None, :] + turned, tensor[..., ROT:]], axis=-1)


def masked_scores(queries, keys_block, query_place, place_block):
    scores = jnp.einsum("qhd,khd->hqk", queries, keys_block, preferred_element_type=jnp.float32) * (
        1.0 / math.sqrt(HEAD_DIM)
    )
    return jnp.where(place_block[None, None, :] <= query_place[None, :, None], scores, MASKED)


def split_blocks(keys_all, values_all, key_place, block_rows):
    blocks = keys_all.shape[0] // block_rows
    key_blocks = keys_all.reshape((blocks, block_rows) + keys_all.shape[1:])
    value_blocks = values_all.reshape((blocks, block_rows) + values_all.shape[1:])
    place_blocks = key_place.reshape(blocks, block_rows)
    return (key_blocks, value_blocks, place_blocks)


def attend_forward(queries, keys_all, values_all, query_place, key_place, block_rows):
    tokens, head_count = (queries.shape[0], queries.shape[1])
    key_blocks, value_blocks, place_blocks = split_blocks(
        keys_all, values_all, key_place, block_rows
    )

    def maxima_step(state_pair, pieces):
        running, totals = state_pair
        keys_block, place_block = pieces
        scores = masked_scores(queries, keys_block, query_place, place_block)
        newest = jnp.maximum(running, jnp.max(scores, axis=-1))
        totals = totals * jnp.exp(running - newest) + jnp.sum(
            jnp.exp(scores - newest[:, :, None]), axis=-1
        )
        return ((newest, totals), None)

    initial = (
        jnp.full((head_count, tokens), MASKED, jnp.float32),
        jnp.zeros((head_count, tokens), jnp.float32),
    )
    (running, totals), ignored = lax.scan(maxima_step, initial, (key_blocks, place_blocks))
    log_total = running + jnp.log(totals)

    def output_step(accumulated, pieces):
        keys_block, values_block, place_block = pieces
        scores = masked_scores(queries, keys_block, query_place, place_block)
        soft_weights = jnp.exp(scores - log_total[:, :, None]).astype(jnp.bfloat16)
        accumulated = accumulated + jnp.einsum(
            "hqk,khd->qhd", soft_weights, values_block, preferred_element_type=jnp.float32
        )
        return (accumulated, None)

    summed, ignored = lax.scan(
        output_step, jnp.zeros(queries.shape, jnp.float32), (key_blocks, value_blocks, place_blocks)
    )
    return (summed.astype(jnp.bfloat16), log_total)


def attend_backward(
    queries,
    keys_all,
    values_all,
    query_place,
    key_place,
    block_rows,
    log_total,
    delta_rows,
    context_grad,
):
    key_blocks, value_blocks, place_blocks = split_blocks(
        keys_all, values_all, key_place, block_rows
    )

    def grad_step(query_sum, pieces):
        keys_block, values_block, place_block = pieces
        scores = masked_scores(queries, keys_block, query_place, place_block)
        exact_probs = jnp.exp(scores - log_total[:, :, None])
        probs_grad = jnp.einsum(
            "qhd,khd->hqk", context_grad, values_block, preferred_element_type=jnp.float32
        )
        score_grad = (
            exact_probs * (probs_grad - delta_rows[:, :, None]) * (1.0 / math.sqrt(HEAD_DIM))
        ).astype(jnp.bfloat16)
        query_sum = query_sum + jnp.einsum(
            "hqk,khd->qhd", score_grad, keys_block, preferred_element_type=jnp.float32
        )
        soft_weights = exact_probs.astype(jnp.bfloat16)
        value_grad = jnp.einsum(
            "hqk,qhd->khd", soft_weights, context_grad, preferred_element_type=jnp.float32
        )
        key_grad = jnp.einsum(
            "hqk,qhd->khd", score_grad, queries, preferred_element_type=jnp.float32
        )
        return (query_sum, (key_grad, value_grad))

    query_grad, gathered_grads = lax.scan(
        grad_step, jnp.zeros(queries.shape, jnp.float32), (key_blocks, value_blocks, place_blocks)
    )
    return (
        query_grad,
        gathered_grads[0].reshape(keys_all.shape),
        gathered_grads[1].reshape(values_all.shape),
    )


def body(
    layer_input,
    out_grad,
    span_order,
    inward,
    inward_bias,
    outward,
    outward_bias,
    expand,
    expand_bias,
    contract,
    contract_bias,
    first_gain,
    first_bias,
    second_gain,
    second_bias,
):
    context_count = lax.axis_size("ctx")
    context_index = lax.axis_index("ctx")
    whole = (
        lax.all_gather(inward, "fsdp", axis=0, tiled=True),
        lax.all_gather(inward_bias, "fsdp", axis=0, tiled=True),
        lax.all_gather(outward, "fsdp", axis=0, tiled=True),
        lax.all_gather(outward_bias, "fsdp", axis=0, tiled=True),
        lax.all_gather(expand, "fsdp", axis=0, tiled=True),
        lax.all_gather(expand_bias, "fsdp", axis=0, tiled=True),
        lax.all_gather(contract, "fsdp", axis=0, tiled=True),
        lax.all_gather(contract_bias, "fsdp", axis=0, tiled=True),
        lax.all_gather(first_gain, "fsdp", axis=0, tiled=True),
        lax.all_gather(first_bias, "fsdp", axis=0, tiled=True),
        lax.all_gather(second_gain, "fsdp", axis=0, tiled=True),
        lax.all_gather(second_bias, "fsdp", axis=0, tiled=True),
    )
    inward_whole, inward_offset, outward_whole, outward_offset = (
        whole[0],
        whole[1].astype(jnp.float32),
        whole[2],
        whole[3].astype(jnp.float32),
    )
    expand_whole, expand_offset, contract_whole, contract_offset = (
        whole[4],
        whole[5].astype(jnp.float32),
        whole[6],
        whole[7].astype(jnp.float32),
    )
    gain_first, offset_first = (whole[8].astype(jnp.float32), whole[9].astype(jnp.float32))
    gain_second, offset_second = (whole[10].astype(jnp.float32), whole[11].astype(jnp.float32))
    tokens = layer_input.shape[1]
    model_width = layer_input.shape[2]
    head_count = model_width // HEAD_DIM
    length = tokens * context_count
    span_size = tokens // 2
    local_place = slot_positions(span_order, context_index * tokens, tokens, span_size)
    key_place = slot_positions(span_order, 0, length, span_size)
    cosine, sine_table = rotary_tables(local_place)
    hidden = layer_input[0].astype(jnp.float32)
    first_float, first_normed, first_inverse = norm_forward(hidden, gain_first, offset_first)
    first_rows = first_float.astype(jnp.bfloat16)
    second_float, second_normed, second_inverse = norm_forward(hidden, gain_second, offset_second)
    second_rows = second_float.astype(jnp.bfloat16)
    projected = (
        jnp.dot(first_rows, inward_whole, preferred_element_type=jnp.float32) + inward_offset
    )
    queries = rotate(
        projected[:, :model_width].reshape(tokens, head_count, HEAD_DIM), cosine, sine_table
    ).astype(jnp.bfloat16)
    keys_local = rotate(
        projected[:, model_width : 2 * model_width].reshape(tokens, head_count, HEAD_DIM),
        cosine,
        sine_table,
    ).astype(jnp.bfloat16)
    values_local = projected[:, 2 * model_width :].astype(jnp.bfloat16)
    pairs_local = jnp.concatenate([keys_local.reshape(tokens, model_width), values_local], axis=1)
    pairs_all = lax.all_gather(pairs_local, "ctx", axis=0, tiled=True)
    keys_all = pairs_all[:, :model_width].reshape(length, head_count, HEAD_DIM)
    values_all = pairs_all[:, model_width:].reshape(length, head_count, HEAD_DIM)
    block_rows = min(512, length)
    context, log_total = attend_forward(
        queries, keys_all, values_all, local_place, key_place, block_rows
    )
    context_rows = context.reshape(tokens, model_width)
    attended = (
        jnp.dot(context_rows, outward_whole, preferred_element_type=jnp.float32) + outward_offset
    )
    before = jnp.dot(second_rows, expand_whole, preferred_element_type=jnp.float32) + expand_offset
    activated = gelu_value(before).astype(jnp.bfloat16)
    mixed = jnp.dot(activated, contract_whole, preferred_element_type=jnp.float32) + contract_offset
    result = (hidden + attended + mixed).astype(jnp.bfloat16)
    grad_rows = out_grad[0]
    grad_float = grad_rows.astype(jnp.float32)
    bias_total = jnp.sum(grad_float, axis=0)
    outward_delta = jnp.dot(context_rows.T, grad_rows, preferred_element_type=jnp.float32)
    contract_delta = jnp.dot(activated.T, grad_rows, preferred_element_type=jnp.float32)
    before_grad = jnp.dot(
        grad_rows, contract_whole.T, preferred_element_type=jnp.float32
    ) * gelu_slope(before)
    expand_sum = jnp.sum(before_grad, axis=0)
    before_rows = before_grad.astype(jnp.bfloat16)
    expand_delta = jnp.dot(second_rows.T, before_rows, preferred_element_type=jnp.float32)
    second_back = jnp.dot(before_rows, expand_whole.T, preferred_element_type=jnp.float32)
    second_input, second_scale, second_shift = norm_backward(
        second_back, second_normed, second_inverse, gain_second
    )
    context_grad = (
        jnp.dot(grad_rows, outward_whole.T, preferred_element_type=jnp.float32)
        .astype(jnp.bfloat16)
        .reshape(tokens, head_count, HEAD_DIM)
    )
    delta_rows = jnp.sum(context_grad.astype(jnp.float32) * context.astype(jnp.float32), axis=-1).T
    query_grad, key_grad, value_grad = attend_backward(
        queries,
        keys_all,
        values_all,
        local_place,
        key_place,
        block_rows,
        log_total,
        delta_rows,
        context_grad,
    )
    pair_terms = jnp.concatenate(
        [key_grad.reshape(length, model_width), value_grad.reshape(length, model_width)], axis=1
    )
    pair_mine = lax.psum_scatter(pair_terms, "ctx", scatter_dimension=0, tiled=True)
    key_rows = pair_mine[:, :model_width]
    value_rows = pair_mine[:, model_width:]
    key_mine = unrotate(key_rows.reshape(tokens, head_count, HEAD_DIM), cosine, sine_table).reshape(
        tokens, model_width
    )
    query_mine = unrotate(query_grad, cosine, sine_table).reshape(tokens, model_width)
    projected_grad = jnp.concatenate([query_mine, key_mine, value_rows], axis=1)
    inward_sum = jnp.sum(projected_grad, axis=0)
    projected_rows = projected_grad.astype(jnp.bfloat16)
    inward_delta = jnp.dot(first_rows.T, projected_rows, preferred_element_type=jnp.float32)
    first_back = jnp.dot(projected_rows, inward_whole.T, preferred_element_type=jnp.float32)
    first_input, first_scale, first_shift = norm_backward(
        first_back, first_normed, first_inverse, gain_first
    )
    input_delta = grad_float + first_input + second_input
    deltas = (
        inward_delta,
        inward_sum,
        outward_delta,
        bias_total,
        expand_delta,
        expand_sum,
        contract_delta,
        bias_total,
        first_scale,
        first_shift,
        second_scale,
        second_shift,
    )
    shards = (
        lax.psum_scatter(deltas[0], "fsdp", scatter_dimension=0, tiled=True),
        lax.psum_scatter(deltas[1], "fsdp", scatter_dimension=0, tiled=True),
        lax.psum_scatter(deltas[2], "fsdp", scatter_dimension=0, tiled=True),
        lax.psum_scatter(deltas[3], "fsdp", scatter_dimension=0, tiled=True),
        lax.psum_scatter(deltas[4], "fsdp", scatter_dimension=0, tiled=True),
        lax.psum_scatter(deltas[5], "fsdp", scatter_dimension=0, tiled=True),
        lax.psum_scatter(deltas[6], "fsdp", scatter_dimension=0, tiled=True),
        lax.psum_scatter(deltas[7], "fsdp", scatter_dimension=0, tiled=True),
        lax.psum_scatter(deltas[8], "fsdp", scatter_dimension=0, tiled=True),
        lax.psum_scatter(deltas[9], "fsdp", scatter_dimension=0, tiled=True),
        lax.psum_scatter(deltas[10], "fsdp", scatter_dimension=0, tiled=True),
        lax.psum_scatter(deltas[11], "fsdp", scatter_dimension=0, tiled=True),
    )
    totals = lax.psum(
        (
            shards[0],
            shards[1],
            shards[2],
            shards[3],
            shards[4],
            shards[5],
            shards[6],
            shards[7],
            shards[8],
            shards[9],
            shards[10],
            shards[11],
        ),
        ("batch", "ctx"),
    )
    return (
        result[None],
        input_delta[None],
        totals[0],
        totals[1],
        totals[2],
        totals[3],
        totals[4],
        totals[5],
        totals[6],
        totals[7],
        totals[8],
        totals[9],
        totals[10],
        totals[11],
    )


def solution(mesh):
    in_specs = (
        P(("batch", "fsdp"), "ctx", None),
        P(("batch", "fsdp"), "ctx", None),
        P(),
        P("fsdp", None),
        P("fsdp"),
        P("fsdp", None),
        P("fsdp"),
        P("fsdp", None),
        P("fsdp"),
        P("fsdp", None),
        P("fsdp"),
        P("fsdp"),
        P("fsdp"),
        P("fsdp"),
        P("fsdp"),
    )
    out_specs = (
        P(("batch", "fsdp"), "ctx", None),
        P(("batch", "fsdp"), "ctx", None),
        P("fsdp", None),
        P("fsdp"),
        P("fsdp", None),
        P("fsdp"),
        P("fsdp", None),
        P("fsdp"),
        P("fsdp", None),
        P("fsdp"),
        P("fsdp"),
        P("fsdp"),
        P("fsdp"),
        P("fsdp"),
    )
    return jax.shard_map(body, mesh=mesh, in_specs=in_specs, out_specs=out_specs, check_vma=False)
```

profile of v0, /device:TPU:0, one launch (start us, length us, event | category | flops | bytes accessed | tf_op | source)
XLA Modules:
  0.0 1527.5 jit_solution(13571899896403762363)
XLA Ops:
  7.3 0.7 all-gather.13.cloned.1.call-update
  8.0 0.7 all-gather.17.cloned.1.call-update
  9.1 5.3 all-gather
  14.3 4.3 all-gather.1
  18.7 4.4 all-gather.2
  23.4 69.3 %all-gather.13.cloned.1.call-done = bf16[1024,3072]{1,0:T(8,128)(2,1)} async-done(((bf16[512,3072]{1,0:T(8,128)(2,1)}), bf16[1024,3072]{1,0:T(8,128)(2,1)}) %all-gather.13.cloned.1.call-update) | async-done | bytes 6291472 | tf_op jit(solution)/shard_map/all_gather | solution.py:201
  92.7 3.9 convolution_add_fusion.1
  97.4 0.8 pad_maximum_fusion.2
  98.3 0.5 all-gather.19.cloned.1.call-update
  98.9 0.5 all-gather.21.cloned.1.call-update
  99.7 27.7 %all-gather.17.cloned.1.call-done = bf16[1024,1024]{1,0:T(8,128)(2,1)} async-done(((bf16[512,1024]{1,0:T(8,128)(2,1)}), bf16[1024,1024]{1,0:T(8,128)(2,1)}) %all-gather.17.cloned.1.call-update) | async-done | bytes 2097168 | tf_op jit(solution)/shard_map/all_gather | solution.py:203
  127.4 2.4 convolution_convert_fusion
  130.1 45.5 %all-gather.15.cloned.1.call-done = bf16[512,2048]{1,0:T(8,128)(2,1)} async-done(((bf16[128,2048]{1,0:T(8,128)(2,1)}), bf16[512,2048]{1,0:T(8,128)(2,1)}) %all-gather.15.cloned.1.call-update) | async-done | bytes 2097168 | tf_op jit(solution)/shard_map/all_gather | solution.py:254
  175.5 2.7 fusion.91
  178.2 1.5 copy.58
  179.7 1.3 copy.56
  181.0 0.9 fusion.1
  182.0 1.2 exponential_reduce_fusion
  183.3 1.3 multiply_reduce_fusion
  184.7 1.8 multiply_convert_fusion
  186.9 0.9 copy-done.2
  187.8 1.3 fusion.54
  189.0 2.5 pad_maximum_fusion
  191.6 2.7 fusion.44
  194.4 0.6 copy-done.21
  195.0 4.3 all-gather.4
  199.3 4.4 all-gather.5
  203.7 4.6 all_gather.49
  208.3 71.6 %all-gather.19.cloned.1.call-done = bf16[1024,4096]{1,0:T(8,128)(2,1)} async-done(((bf16[512,4096]{1,0:T(8,128)(2,1)}), bf16[1024,4096]{1,0:T(8,128)(2,1)}) %all-gather.19.cloned.1.call-update) | async-done | bytes 8388624 | tf_op jit(solution)/shard_map/all_gather | solution.py:205
  279.9 4.8 convolution_add_fusion
  284.7 10.5 fusion.42
  295.3 90.0 %all-gather.21.cloned.1.call-done = bf16[4096,1024]{1,0:T(8,128)(2,1)} async-done(((bf16[2048,1024]{1,0:T(8,128)(2,1)}), bf16[4096,1024]{1,0:T(8,128)(2,1)}) %all-gather.21.cloned.1.call-update) | async-done | bytes 8388624 | tf_op jit(solution)/shard_map/all_gather | solution.py:207
  385.3 6.6 fusion.96
  391.9 1.0 copy-done.9
  392.9 8.2 fusion.38
  401.1 2.4 convolution_bitcast_fusion
  403.6 0.8 copy-done.10
  404.3 60.5 %reduce-scatter.6.cloned.1.call-done = f32[128,2048]{0,1:T(8,128)} async-done(((f32[512,2048]{0,1:T(8,128)}), f32[128,2048]{0,1:T(8,128)}) %reduce-scatter.6.cloned.1.call-update) | async-done | bytes 1048592 | tf_op jit(solution)/shard_map/reduce_scatter | solution.py:304
  464.8 1.3 fusion.93
  466.4 0.5 copy-done.4
  466.9 6.4 fusion.81
  473.4 49.2 %reduce-scatter.10.cloned.1.call-done = f32[512,1024]{1,0:T(8,128)} async-done(((f32[1024,1024]{1,0:T(8,128)}), f32[512,1024]{1,0:T(8,128)}) %reduce-scatter.10.cloned.1.call-update) | async-done | bytes 2097168 | tf_op jit(solution)/shard_map/reduce_scatter | solution.py:337
  522.6 191.5 %reduce-scatter.14.cloned.1.call-done = f32[2048,1024]{1,0:T(8,128)} async-done(((f32[4096,1024]{1,0:T(8,128)}), f32[2048,1024]{1,0:T(8,128)}) %reduce-scatter.14.cloned.1.call-update) | async-done | bytes 8388624 | tf_op jit(solution)/shard_map/reduce_scatter | solution.py:341
  714.1 191.6 %reduce-scatter.12.cloned.1.call-done = f32[512,4096]{1,0:T(8,128)} async-done(((f32[1024,4096]{1,0:T(8,128)}), f32[512,4096]{1,0:T(8,128)}) %reduce-scatter.12.cloned.1.call-update) | async-done | bytes 8388624 | tf_op jit(solution)/shard_map/reduce_scatter | solution.py:339
  905.6 146.6 %reduce-scatter.8.cloned.1.call-done = f32[512,3072]{1,0:T(8,128)} async-done(((f32[1024,3072]{1,0:T(8,128)}), f32[512,3072]{1,0:T(8,128)}) %reduce-scatter.8.cloned.1.call-update) | async-done | bytes 6291472 | tf_op jit(solution)/shard_map/reduce_scatter | solution.py:335
  1052.3 0.6 copy-done.26
  1052.9 0.6 dynamic-slice.1
  1055.5 4.3 all-gather.3
  1059.9 4.6 all-gather.6
  1064.4 6.8 fusion.40
  1071.2 5.0 convolution_add_fusion.3
  1076.3 1.2 fusion.9
  1077.5 0.5 fusion.10
  1078.0 2.5 fusion.35
  1080.6 1.2 convert_reduce_fusion
  1081.8 7.6 all-reduce.9
  1089.8 63.7 %all-reduce.7 = (f32[1536]{0:T(1024)}, f32[512]{0:T(512)S(1)}, f32[2048]{0:T(1024)}, f32[512]{0:T(512)}, f32[512]{0:T(512)}, /*index=5*/f32[512]{0:T(512)}, f32[512]{0:T(512)}) all-reduce(f32[1536]{0:T(1024)S(1)} %dynamic-slice.2, f32[512]{0:T(512)S(1)} %dynamic-slice.4, ...), channel_id=1, replica_groups=mesh['batch'=4,'ctx'=4,'fsdp'=2] {'batch','ctx'}, use_global_device_ids=true, to_apply=%region_16.17 | all-reduce | flops 6144 | bytes 49152 | tf_op jit(solution)/shard_map/psum | solution.py:348
  1153.6 349.0 %all-reduce.12.cloned.1.call-done = (f32[512,3072]{1,0:T(8,128)}, f32[512,1024]{1,0:T(8,128)}, f32[512,4096]{1,0:T(8,128)}, f32[2048,1024]{1,0:T(8,128)}) async-done(((f32[512,3072]{1,0:T(8,128)}, f32[512,1024]{1,0:T(8,128)}, f32[512,4096]{1,0:T(8,128)}, f32[2048,1024]{1,0:T(8,128)}), (f32[512,3072]{1,0:T(8,128)}, f32[512,1024]{1,0:T(8,128)}, f32[512,4096]{1,0:T(8,128)}, ...) | async-done | bytes 25165840 | tf_op jit(solution)/shard_map/psum | solution.py:348
  1502.6 0.6 copy.65
  1503.2 6.9 copy.66
  1510.0 1.3 copy.67
  1511.8 4.3 copy.68
  1516.0 1.5 slice-done.3
  1517.5 3.4 copy.69
  (138 shorter events, 4.2 us)
Async XLA Ops:
  7.2 1.6 copy-start
  7.2 1.7 copy-start.25
  7.2 1.8 copy-start.19
  7.2 7.1 copy-start.20
  7.2 11.5 copy-start.17
  7.2 85.5 %all-gather.13.cloned.1.call-start = ((), (), s32[]{:S(2)}) async-start(), calls=%async_computation.5 | async-start | bytes 9437184 | tf_op jit(solution)/shard_map/all_gather | solution.py:201
  8.0 119.4 %all-gather.17.cloned.1.call-start = ((), (), s32[]{:S(2)}) async-start(), calls=%async_computation.7 | async-start | bytes 3145728 | tf_op jit(solution)/shard_map/all_gather | solution.py:203
  8.7 166.8 %all-gather.15.cloned.1.call-start = ((), (), s32[]{:S(2)}) async-start(), calls=%async_computation.6 | async-start | bytes 2621440 | tf_op jit(solution)/shard_map/all_gather | solution.py:254
  98.3 181.6 %all-gather.19.cloned.1.call-start = ((), (), s32[]{:S(2)}) async-start(), calls=%async_computation.8 | async-start | bytes 12582912 | tf_op jit(solution)/shard_map/all_gather | solution.py:205
  98.9 28.6 %copy-start.6 = (bf16[1,128,1024]{2,1,0:T(8,128)(2,1)S(1)}, bf16[1,128,1024]{2,1,0:T(8,128)(2,1)}, u32[]{:S(2)}) copy-start(bf16[1,128,1024]{2,1,0:T(8,128)(2,1)} %param.16) | copy-start | bytes 786436
  98.9 286.4 %all-gather.21.cloned.1.call-start = ((), (), s32[]{:S(2)}) async-start(), calls=%async_computation.9 | async-start | bytes 12582912 | tf_op jit(solution)/shard_map/all_gather | solution.py:207
  99.5 365.4 %reduce-scatter.6.cloned.1.call-start = ((), (), s32[]{:S(2)}) async-start(), calls=%async_computation.10 | async-start | bytes 5242880 | tf_op jit(solution)/shard_map/reduce_scatter | solution.py:304
  181.9 1.4 copy-start.13
  184.7 6.9 copy-start.14
  186.5 1.3 copy-start.2
  191.5 331.1 %reduce-scatter.10.cloned.1.call-start = ((), (), s32[]{:S(2)}) async-start(), calls=%async_computation.12 | async-start | bytes 6291456 | tf_op jit(solution)/shard_map/reduce_scatter | solution.py:337
  194.3 0.7 copy-start.21
  194.3 5.0 copy-start.22
  194.3 9.4 copy-start.16
  194.3 519.8 %reduce-scatter.14.cloned.1.call-start = ((), (), s32[]{:S(2)}) async-start(), calls=%async_computation.14 | async-start | bytes 25165824 | tf_op jit(solution)/shard_map/reduce_scatter | solution.py:341
  279.9 4.8 copy-start.7
  295.2 610.4 %reduce-scatter.12.cloned.1.call-start = ((), (), s32[]{:S(2)}) async-start(), calls=%async_computation.13 | async-start | bytes 25165824 | tf_op jit(solution)/shard_map/reduce_scatter | solution.py:339
  391.9 1.0 copy-start.9
  401.1 651.2 %reduce-scatter.8.cloned.1.call-start = ((), (), s32[]{:S(2)}) async-start(), calls=%async_computation.11 | async-start | bytes 18874368 | tf_op jit(solution)/shard_map/reduce_scatter | solution.py:335
  403.5 0.8 copy-start.10
  404.3 61.9 %copy-start.11 = (f32[128,16,64]{0,2,1:T(8,128)S(1)}, f32[128,16,64]{0,2,1:T(8,128)}, u32[]{:S(2)}) copy-start(f32[128,16,64]{0,2,1:T(8,128)} %copy-done.10) | copy-start | bytes 1572868
  464.8 1.5 slice-start.4
  466.1 0.8 copy-start.4
  473.4 1029.2 %all-reduce.12.cloned.1.call-start = ((), (), s32[]{:S(2)}) async-start(), calls=%async_computation.15 | async-start | bytes 50331648 | tf_op jit(solution)/shard_map/psum | solution.py:348
  1052.3 0.7 copy-start.26
  1052.3 3.2 copy-start.23
  1052.3 7.5 copy-start.24
  1064.4 13.5 slice-start
  1071.2 5.1 copy-start.1
  1071.2 5.1 copy-start.15
  1071.2 6.8 slice-start.1
  1076.2 1.2 copy-start.5
  1078.0 2.6 copy-start.8
  1153.6 356.5 %copy-start.18 = (f32[512]{0:T(512)}, f32[512]{0:T(512)S(1)}, u32[]{:S(2)}) copy-start(f32[512]{0:T(512)S(1)} %get-tuple-element.195) | copy-start | bytes 6148
  1503.2 6.9 copy-start.12
  1503.2 8.6 copy-start.3
  1510.0 6.0 slice-start.2
  1511.8 5.8 slice-start.3
Sparse Core Ops, SparseCore 0:
  9.6 83.0 all-gather.12
  94.3 33.1 all-gather.16
  129.6 45.9 all-gather.14
  176.9 102.8 all-gather.18
  281.2 103.9 all-gather.20
  388.0 76.7 reduce-scatter.5
  467.8 54.7 reduce-scatter.9
  524.9 189.1 reduce-scatter.13
  716.5 189.1 reduce-scatter.11
  907.8 144.4 reduce-scatter.7
  1057.2 445.3 all-reduce.11
where the time goes:
time: 1530 us
  waiting for transfers between devices  1290 us (84%)
  blocking collectives  107 us (7%)
  matrix products  69.1 us (5%)
  local copies, waits for them, and re-layouts  31.7 us (2%)
  between operations  16.5 us (1%)
    psum x1, waiting for transfers between devices, body(): lax.psum((shards[0], shards[1], shards[2], shards[3], shards[4], shards[5...  349 us
    reduce_scatter x1, waiting for transfers between devices, body(): lax.psum_scatter(deltas[4], 'fsdp', scatter_dimension=0, tiled=True)  192 us
    reduce_scatter x1, waiting for transfers between devices, body(): lax.psum_scatter(deltas[6], 'fsdp', scatter_dimension=0, tiled=True)  191 us
    reduce_scatter x1, waiting for transfers between devices, body(): lax.psum_scatter(deltas[0], 'fsdp', scatter_dimension=0, tiled=True)  147 us
    all_gather x1, waiting for transfers between devices, body(): lax.all_gather(contract, 'fsdp', axis=0, tiled=True)  90 us
    all_gather x1, waiting for transfers between devices, body(): lax.all_gather(expand, 'fsdp', axis=0, tiled=True)  71.6 us
    all_gather x1, waiting for transfers between devices, body(): lax.all_gather(inward, 'fsdp', axis=0, tiled=True)  69.3 us
    psum x1, blocking collectives, body(): lax.psum((shards[0], shards[1], shards[2], shards[3], shards[4], shards[5...  63.7 us
  transfers between devices with their start and end apart: 11, of which 11 were waited for; matrix products, arithmetic and copies ran while one was open for 6% of the time, Pallas kernels for 0%

commit v1 on v0

v1 whole, which is shorter than its diff:
```python
import math

import jax
import jax.numpy as jnp
from jax import lax
from jax.sharding import PartitionSpec as P

HEAD_DIM = 64
ROT = 16

EPSILON = 1e-05
ROTARY_BASE = 10000.0
MASKED = -1e30
HALF_ROOT = 0.7071067811865476
NORMAL_PEAK = 0.3989422804014327
PLANE = ("batch", "fsdp")


def dot(left, right, contract=((1,), (0,))):
    return lax.dot_general(left, right, (contract, ((), ())), preferred_element_type=jnp.float32)


def normalize(values):
    center = values - jnp.mean(values, axis=-1, keepdims=True)
    inverse = lax.rsqrt(jnp.mean(center * center, axis=-1, keepdims=True) + EPSILON)
    return (center * inverse, inverse)


def norm_backward(upstream, normed, inverse, factor):
    scaled = upstream * factor
    middle = jnp.mean(scaled, axis=-1, keepdims=True)
    coupled = jnp.mean(scaled * normed, axis=-1, keepdims=True)
    result = inverse * (scaled - middle - normed * coupled)
    return (result, jnp.sum(upstream * normed, axis=0), jnp.sum(upstream, axis=0))


def slot_positions(span_order, first_slot, slot_count, span_size):
    slot_index = first_slot + jnp.arange(slot_count, dtype=jnp.int32)
    owners = slot_index // (2 * span_size)
    places = jnp.arange(span_order.shape[0], dtype=jnp.int32)
    leading = jnp.sum(jnp.where(owners[:, None] == places[None, :], span_order[None, :], 0), axis=1)
    spans = 2 * span_order.shape[0]
    picked = jnp.where(slot_index // span_size % 2 == 0, leading, spans - 1 - leading)
    return picked * span_size + slot_index % span_size


def rotary_tables(positions):
    half_rot = ROT // 2
    angular = jnp.exp(
        jnp.arange(half_rot, dtype=jnp.float32) * (-2.0 * math.log(ROTARY_BASE) / ROT)
    )
    angles = positions.astype(jnp.float32)[:, None] * angular[None, :]
    angles = jnp.concatenate([angles, angles], axis=1)
    return (jnp.cos(angles), jnp.sin(angles))


def rotate(tensor, cosine, sine_table):
    half_rot = ROT // 2
    leading_part = tensor[..., :ROT]
    turned = jnp.concatenate([-leading_part[..., half_rot:], leading_part[..., :half_rot]], axis=-1)
    rotated = leading_part * cosine[:, None, :] + turned * sine_table[:, None, :]
    return jnp.concatenate([rotated, tensor[..., ROT:]], axis=-1)


def unrotate(tensor, cosine, sine_table):
    half_rot = ROT // 2
    leading_part = tensor[..., :ROT]
    weighted = leading_part * sine_table[:, None, :]
    turned = jnp.concatenate([weighted[..., half_rot:], -weighted[..., :half_rot]], axis=-1)
    return jnp.concatenate([leading_part * cosine[:, None, :] + turned, tensor[..., ROT:]], axis=-1)


def attention(mixed, place, cosine, sine_table, heads):
    sequences, length, _ = mixed.shape
    parts = mixed.reshape(sequences, length, 4, heads, HEAD_DIM)
    queries, keys, values, grads = (parts[:, :, i] for i in range(4))
    scale = 1.0 / math.sqrt(HEAD_DIM)
    scores = jnp.einsum("sqhd,skhd->shqk", queries, keys, preferred_element_type=jnp.float32)
    allowed = place[None, :] <= place[:, None]
    scores = jnp.where(allowed, scores * scale, MASKED)
    peak = jnp.max(scores, axis=-1, keepdims=True)
    log_total = peak + jnp.log(jnp.sum(jnp.exp(scores - peak), axis=-1, keepdims=True))
    probs = jnp.exp(scores - log_total)
    soft = probs.astype(jnp.bfloat16)
    context = jnp.einsum("shqk,skhd->sqhd", soft, values, preferred_element_type=jnp.float32)
    context = context.astype(jnp.bfloat16)
    delta = jnp.einsum(
        "sqhd,sqhd->shq", grads.astype(jnp.float32), context.astype(jnp.float32)
    )
    value_grad = jnp.einsum("shqk,sqhd->skhd", soft, grads, preferred_element_type=jnp.float32)
    probs_grad = jnp.einsum("sqhd,skhd->shqk", grads, values, preferred_element_type=jnp.float32)
    score_grad = (probs * (probs_grad - delta[..., None]) * scale).astype(jnp.bfloat16)
    query_grad = jnp.einsum("shqk,skhd->sqhd", score_grad, keys, preferred_element_type=jnp.float32)
    key_grad = jnp.einsum("shqk,sqhd->skhd", score_grad, queries, preferred_element_type=jnp.float32)
    query_grad = unrotate(query_grad, cosine, sine_table)
    key_grad = unrotate(key_grad, cosine, sine_table)
    back = jnp.stack([query_grad, key_grad, value_grad], axis=2)
    shift = jnp.sum(back, axis=(0, 1)).reshape(-1)
    full = jnp.concatenate([context[:, :, None], back.astype(jnp.bfloat16)], axis=2)
    return (full.reshape(sequences, length, 4 * heads * HEAD_DIM), shift)


def body(
    layer_input,
    out_grad,
    span_order,
    inward,
    inward_bias,
    outward,
    outward_bias,
    expand,
    expand_bias,
    contract,
    contract_bias,
    first_gain,
    first_bias,
    second_gain,
    second_bias,
):
    batch_count, fsdp_count = (lax.axis_size("batch"), lax.axis_size("fsdp"))
    context_count = lax.axis_size("ctx")
    context_index = lax.axis_index("ctx")
    batch_index, fsdp_index = (lax.axis_index("batch"), lax.axis_index("fsdp"))
    plane = batch_count * fsdp_count
    tokens, width = layer_input.shape[1:]
    hidden_units = expand.shape[1]
    head_cols = width // plane
    unit_cols = hidden_units // plane
    heads = head_cols // HEAD_DIM
    length = tokens * context_count
    span_size = tokens // 2
    own_sequences = plane // context_count

    def full_vectors(*vectors):
        sizes = [v.shape[0] for v in vectors]
        gathered = lax.all_gather(jnp.concatenate(vectors), "fsdp")
        out, start = ([], 0)
        for size in sizes:
            out.append(gathered[:, start : start + size].reshape(-1).astype(jnp.float32))
            start += size
        return out

    (
        inward_offset,
        outward_offset,
        expand_offset,
        contract_offset,
        gain_first,
        offset_first,
        gain_second,
        offset_second,
    ) = full_vectors(
        inward_bias,
        outward_bias,
        expand_bias,
        contract_bias,
        first_gain,
        first_bias,
        second_gain,
        second_bias,
    )

    def chunk(array, cols):
        rows = array.shape[0]
        parts = array.reshape(rows, -1, fsdp_count, batch_count, cols)
        mine = lax.dynamic_index_in_dim(parts, batch_index, 3, keepdims=False)
        return mine.transpose(2, 0, 1, 3).reshape(fsdp_count, rows, -1)

    to_send = jnp.concatenate([chunk(inward, head_cols), chunk(expand, unit_cols)], axis=2)
    weights = lax.all_to_all(to_send, "fsdp", 0, 0).reshape(width, -1)
    inward_cols = weights[:, : 3 * head_cols]
    expand_cols = weights[:, 3 * head_cols :]
    outward_rows = lax.dynamic_slice_in_dim(outward, batch_index * head_cols, head_cols, 0)
    contract_rows = lax.dynamic_slice_in_dim(contract, batch_index * unit_cols, unit_cols, 0)
    plane_index = fsdp_index * batch_count + batch_index
    inward_shift_in = lax.dynamic_index_in_dim(
        inward_offset.reshape(3, plane, head_cols), plane_index, 1, keepdims=False
    ).reshape(-1)
    expand_shift_in = lax.dynamic_slice_in_dim(expand_offset, plane_index * unit_cols, unit_cols, 0)

    pair = jnp.stack([layer_input[0], out_grad[0]])
    pair_all = lax.all_gather(pair, PLANE, axis=1, tiled=True)
    grads_all = pair_all[1]
    normed, _ = normalize(pair_all[0].astype(jnp.float32))
    first_rows = (normed * gain_first + offset_first).astype(jnp.bfloat16)
    second_rows = (normed * gain_second + offset_second).astype(jnp.bfloat16)

    local_place = slot_positions(span_order, context_index * tokens, tokens, span_size)
    cosine, sine_table = rotary_tables(local_place)
    cosine_plane = jnp.tile(cosine, (plane, 1))
    sine_plane = jnp.tile(sine_table, (plane, 1))
    projected = dot(first_rows, inward_cols) + inward_shift_in
    projected = projected.reshape(plane * tokens, 3 * heads, HEAD_DIM)
    turned = rotate(projected[:, : 2 * heads], cosine_plane, sine_plane)
    context_grad = dot(grads_all, outward_rows, ((1,), (1,)))
    mixed = jnp.concatenate(
        [
            turned.reshape(plane * tokens, -1),
            projected[:, 2 * heads :].reshape(plane * tokens, -1),
            context_grad,
        ],
        axis=1,
    ).astype(jnp.bfloat16)
    mixed = mixed.reshape(context_count, own_sequences, tokens, 4 * head_cols)
    mixed = lax.all_to_all(mixed, "ctx", 0, 0)
    mixed = mixed.transpose(1, 0, 2, 3).reshape(own_sequences, length, 4 * head_cols)
    place = slot_positions(span_order, 0, length, span_size)
    cosine_all, sine_all = rotary_tables(place)
    back, inward_sum = attention(mixed, place, cosine_all, sine_all, heads)
    back = back.reshape(own_sequences, context_count, tokens, 4 * head_cols).transpose(1, 0, 2, 3)
    back = lax.all_to_all(back, "ctx", 0, 0).reshape(plane * tokens, 4 * head_cols)
    context_rows = back[:, :head_cols]
    projected_rows = back[:, head_cols:]

    before = dot(second_rows, expand_cols) + expand_shift_in
    tail = 1.0 + lax.erf(before * HALF_ROOT)
    activated = (0.5 * before * tail).astype(jnp.bfloat16)
    slope = 0.5 * tail + before * jnp.exp(-0.5 * before * before) * NORMAL_PEAK
    before_grad = dot(grads_all, contract_rows, ((1,), (1,))) * slope
    expand_sum = jnp.sum(before_grad, axis=0)
    before_rows = before_grad.astype(jnp.bfloat16)

    expand_delta = dot(second_rows, before_rows, ((0,), (0,)))
    contract_delta = dot(activated, grads_all, ((0,), (0,)))
    inward_delta = dot(first_rows, projected_rows, ((0,), (0,)))
    outward_delta = dot(context_rows, grads_all, ((0,), (0,)))

    out_part = dot(activated, contract_rows) + dot(context_rows, outward_rows)
    second_part = dot(before_rows, expand_cols, ((1,), (1,)))
    first_part = dot(projected_rows, inward_cols, ((1,), (1,)))
    stacked = jnp.stack([out_part, second_part, first_part], axis=1).astype(jnp.bfloat16)
    mine = lax.psum_scatter(stacked, PLANE, scatter_dimension=0, tiled=True).astype(jnp.float32)

    hidden = layer_input[0].astype(jnp.float32)
    grad_float = out_grad[0].astype(jnp.float32)
    normed_mine, inverse_mine = normalize(hidden)
    result = (hidden + (mine[:, 0] + outward_offset) + contract_offset).astype(jnp.bfloat16)
    second_input, second_scale, second_shift = norm_backward(
        mine[:, 1], normed_mine, inverse_mine, gain_second
    )
    first_input, first_scale, first_shift = norm_backward(
        mine[:, 2], normed_mine, inverse_mine, gain_first
    )
    input_delta = grad_float + first_input + second_input

    columns = jnp.concatenate([inward_delta, expand_delta], axis=1).astype(jnp.bfloat16)
    rows = jnp.concatenate([outward_delta, contract_delta], axis=0).astype(jnp.bfloat16)
    columns, rows = lax.psum((columns, rows), "ctx")
    half = width // fsdp_count
    columns = lax.all_to_all(columns.reshape(fsdp_count, half, -1), "fsdp", 0, 0)
    columns = lax.all_gather(columns, "batch")
    rows = lax.all_gather(rows, "batch")
    columns = columns.transpose(2, 1, 0, 3).astype(jnp.float32)
    inward_total = columns[..., : 3 * head_cols].reshape(
        half, fsdp_count, batch_count, 3, head_cols
    )
    inward_total = inward_total.transpose(0, 3, 1, 2, 4).reshape(half, 3 * width)
    expand_total = columns[..., 3 * head_cols :].reshape(half, hidden_units)
    rows = rows.astype(jnp.float32)
    outward_total = rows[:, :head_cols].reshape(half, width)
    contract_total = rows[:, head_cols:].reshape(-1, width)

    inward_wide = jnp.zeros((3, plane, head_cols), jnp.float32)
    inward_wide = lax.dynamic_update_index_in_dim(
        inward_wide, inward_sum.reshape(3, head_cols), plane_index, 1
    ).reshape(-1)
    expand_wide = jnp.zeros((plane, unit_cols), jnp.float32)
    expand_wide = lax.dynamic_update_index_in_dim(expand_wide, expand_sum, plane_index, 0).reshape(-1)
    bias_total = jnp.sum(grad_float, axis=0)
    vectors = [
        inward_wide,
        bias_total,
        expand_wide,
        first_scale,
        first_shift,
        second_scale,
        second_shift,
    ]
    whole = lax.psum(jnp.concatenate(vectors), ("batch", "ctx", "fsdp"))
    halves, start = ([], 0)
    for vector in vectors:
        part = vector.shape[0] // fsdp_count
        halves.append(lax.dynamic_slice_in_dim(whole, start + fsdp_index * part, part, 0))
        start += vector.shape[0]
    return (
        result[None],
        input_delta[None],
        inward_total,
        halves[0],
        outward_total,
        halves[1],
        expand_total,
        halves[2],
        contract_total,
        halves[1],
        halves[3],
        halves[4],
        halves[5],
        halves[6],
    )


def solution(mesh):
    rows = P(PLANE, "ctx", None)
    matrix, vector = (P("fsdp", None), P("fsdp"))
    in_specs = (rows, rows, P()) + (matrix, vector) * 4 + (vector,) * 4
    out_specs = (rows, rows) + (matrix, vector) * 4 + (vector,) * 4
    return jax.shard_map(body, mesh=mesh, in_specs=in_specs, out_specs=out_specs, check_vma=False)
```

time: 1530 us -> 527 us (0.34)
  waiting for transfers between devices: 1290 us -> 222 us
  local copies, waits for them, and re-layouts: 31.7 us -> 99.2 us
  matrix products: 69.1 us -> 35.2 us
  other arithmetic: 7.33 us -> 32.1 us
    reduce_scatter x5 -> x1, waiting for transfers between devices: 639 us -> 35.8 us  [body(): lax.psum_scatter(stacked, PLANE, scatter_dimension=0, tiled=True)]
    all_gather x5 -> x3, waiting for transfers between devices: 304 us -> 41.3 us  [the longest x1 41.2 us: body(): columns = lax.all_gather(columns, 'batch')]
    psum x1, waiting for transfers between devices: 349 us -> 109 us  [body(): columns, rows = lax.psum((columns, rows), 'ctx')]
    all_to_all x0 -> x3, waiting for transfers between devices: none -> 35.4 us  [the longest x1 23.4 us: body(): mixed = lax.all_to_all(mixed, 'ctx', 0, 0)]
    dot_general x18, matrix products: 69.1 us -> 35.2 us  [the longest x12 28.8 us: dot(): lax.dot_general(left, right, (contract, ((), ())), preferred_element_type...]
    slice x8 -> x9, local copies, waits for them, and re-layouts: 7.31 us -> 40.2 us  [the longest x2 17.7 us: body(): expand_total = columns[..., 3 * head_cols:].reshape(half, hidden_units)]
    all_to_all x0 -> x1, blocking collectives: none -> 27.8 us  [body(): lax.all_to_all(columns.reshape(fsdp_count, half, -1), 'fsdp', 0, 0)]
    psum x1, blocking collectives: 63.7 us -> 40.1 us  [body(): whole = lax.psum(jnp.concatenate(vectors), ('batch', 'ctx', 'fsdp'))]
  transfers between devices with their start and end apart: 11 -> 8, of which waited for: 11 -> 5; matrix products, arithmetic and copies ran while one was open for 6% -> 12% of each run, Pallas kernels for 0% -> 0%
where the time goes in v1:
time: 527 us; the launch traced here: 518 us
  waiting for transfers between devices  222 us (42%)
  blocking collectives  101 us (19%)
  local copies, waits for them, and re-layouts  99.2 us (19%)
  matrix products  35.2 us (7%)
  other arithmetic  32.1 us (6%)
  between operations  15.2 us (3%)
  starting transfers between devices  13.5 us (3%)
    psum x1, waiting for transfers between devices, body(): columns, rows = lax.psum((columns, rows), 'ctx')  109 us
    all_gather x1, waiting for transfers between devices, body(): columns = lax.all_gather(columns, 'batch')  41.2 us
    psum x1, blocking collectives, body(): whole = lax.psum(jnp.concatenate(vectors), ('batch', 'ctx', 'fsdp'))  40.1 us
    reduce_scatter x1, waiting for transfers between devices, body(): lax.psum_scatter(stacked, PLANE, scatter_dimension=0, tiled=True)  35.8 us
    all_gather x1, blocking collectives, full_vectors(): gathered = lax.all_gather(jnp.concatenate(vectors), 'fsdp')  33.3 us
    unnamed x104, local copies, waits for them, and re-layouts  30.7 us
    dot_general x12, matrix products, dot(): lax.dot_general(left, right, (contract, ((), ())), preferred_element_type...  28.8 us
    all_to_all x1, blocking collectives, body(): lax.all_to_all(columns.reshape(fsdp_count, half, -1), 'fsdp', 0, 0)  27.8 us
  transfers between devices with their start and end apart: 8, of which 5 were waited for; matrix products, arithmetic and copies ran while one was open for 12% of the time, Pallas kernels for 0%

profile of v1, /device:TPU:0, one launch (start us, length us, event | category | flops | bytes accessed | tf_op | source)
XLA Modules:
  0.0 518.3 jit_solution(7067339631886443324)
XLA Ops:
  7.2 2.0 pad_maximum_fusion.6
  9.2 6.4 %copy.130 = bf16[512,4096]{0,1:T(8,128)(2,1)} copy(bf16[512,4096]{1,0:T(8,128)(2,1)} %param.22) | data formatting | bytes 8388608 | tf_op args[7]
  15.6 1.3 constant_dynamic-slice_fusion
  17.5 4.7 copy.127
  22.2 1.2 dynamic-slice_bitcast_fusion
  23.4 1.0 copy.129
  24.4 1.6 copy.132
  26.0 1.4 pad_maximum_fusion.1
  27.4 4.3 all-to-all-start
  33.1 33.3 %all-gather.2 = bf16[2,1,6656]{2,1,0:T(2,128)(2,1)S(1)} all-gather(bf16[1,1,6656]{2,1,0:T(2,128)(2,1)S(1)} %reshape.683), channel_id=2, replica_groups=mesh['batch'=4,'ctx'=4,'fsdp'=2] {'fsdp'}, dimensions={0}, use_global_device_ids=true | all-gather | bytes 39936 | tf_op jit(solution)/shard_map/all_gather | solution.py:136
  67.7 1.9 convert_reduce_fusion
  69.6 2.3 fusion.9
  71.9 3.6 convolution_add_fusion
  75.8 0.8 pad_maximum_fusion.7
  76.7 2.2 concatenate.75
  78.9 0.9 concatenate.76
  79.7 0.8 convolution_convert_fusion.3
  80.9 1.5 pad_maximum_fusion.4
  82.5 1.7 copy.134
  84.1 5.3 %all-to-all-start.1 = ((bf16[4,2,128,512]{2,1,3,0:T(2,128)(2,1)}), bf16[4,2,128,512]{2,1,3,0:T(2,128)(2,1)S(1)}, u32[]{:S(2)}, u32[]{:S(2)}) async-start(bf16[4,2,128,512]{2,1,3,0:T(2,128)(2,1)} %copy.134), calls=%async_computation.1 | async-start | bytes 2097152 | tf_op jit(solution)/shard_map/all_to_all | solution.py:205
  90.7 23.4 %all-to-all-done.1 = bf16[4,2,128,512]{2,1,3,0:T(2,128)(2,1)S(1)} async-done(((bf16[4,2,128,512]{2,1,3,0:T(2,128)(2,1)}), bf16[4,2,128,512]{2,1,3,0:T(2,128)(2,1)S(1)}, u32[]{:S(2)}, u32[]{:S(2)}) %all-to-all-start.1) | async-done | bytes 1048608 | tf_op jit(solution)/shard_map/all_to_all | solution.py:205
  114.2 0.8 copy.135
  115.4 0.9 fusion.11
  116.3 0.9 exponential_reduce_fusion
  117.3 1.3 fusion.68
  118.6 1.6 multiply_convert_fusion
  120.7 0.7 convolution_bitcast_fusion.1
  121.4 1.3 convolution_bitcast_fusion
  123.0 0.8 copy-done.4
  124.1 1.1 reshape_reshape.8
  125.2 2.3 copy.146
  127.6 3.5 all-to-all-start.2
  131.4 3.7 multiply_convert_fusion.1
  135.0 2.3 fusion.26
  137.3 3.4 fusion.125
  140.7 1.0 copy-done.37
  141.7 2.6 convolution_convert_fusion
  144.3 12.0 %all-to-all-done.2 = bf16[4,2,128,512]{2,3,1,0:T(8,128)(2,1)S(1)} async-done(((bf16[4,2,128,512]{2,3,1,0:T(8,128)(2,1)}), bf16[4,2,128,512]{2,3,1,0:T(8,128)(2,1)S(1)}, u32[]{:S(2)}, u32[]{:S(2)}) %all-to-all-start.2) | async-done | bytes 1048608 | tf_op jit(solution)/shard_map/all_to_all | solution.py:211
  156.3 1.3 copy.147
  157.6 3.1 convolution_convert_fusion.1
  160.9 2.5 copy.168
  163.4 2.3 fusion.29
  165.6 2.4 maximum_bitcast_fusion
  168.1 2.6 convert_bitcast_fusion.3
  170.8 1.3 convert_bitcast_fusion.2
  172.8 2.5 fusion.23
  175.3 3.1 pad_maximum_fusion
  178.5 109.4 %all-reduce.3.cloned.1.call-done = (bf16[1,640,1024]{2,1,0:T(8,128)(2,1)}, bf16[2,512,896]{2,1,0:T(8,128)(2,1)}) async-done(((bf16[1,640,1024]{2,1,0:T(8,128)(2,1)}, bf16[2,512,896]{2,1,0:T(8,128)(2,1)}), (bf16[1,640,1024]{2,1,0:T(8,128)(2,1)}, bf16[2,512,896]{2,1,0:T(8,128)(2,1)})) %all-reduce.3.cloned.1.call-update) | async-done | bytes 3145744 | tf_op jit(solution)/shard_map/psum | solution.py:248
  288.0 27.8 %all_to_all.20 = bf16[2,512,896]{2,1,0:T(8,128)(2,1)} all-to-all(bf16[2,512,896]{2,1,0:T(8,128)(2,1)} %get-tuple-element.93), channel_id=1, replica_groups=mesh['batch'=4,'ctx'=4,'fsdp'=2] {'fsdp'}, dimensions={0} | all-to-all | bytes 3670016 | tf_op jit(solution)/shard_map/all_to_all | solution.py:250
  316.9 35.8 %reduce-scatter.2.cloned.1.call-done = bf16[128,3,1024]{2,0,1:T(8,128)(2,1)} async-done(((bf16[1024,3,1024]{2,0,1:T(8,128)(2,1)}), bf16[128,3,1024]{2,0,1:T(8,128)(2,1)}) %reduce-scatter.2.cloned.1.call-update) | async-done | bytes 786448 | tf_op jit(solution)/shard_map/reduce_scatter | solution.py:232
  352.7 1.3 convert_element_type.182
  354.5 1.3 fusion.43
  355.9 40.1 %psum.22 = f32[12288]{0:T(1024)S(1)} all-reduce(f32[12288]{0:T(1024)S(1)} %constant_dynamic-update-slice_fusion.2), channel_id=1, replica_groups=mesh['batch'=4,'ctx'=4,'fsdp'=2] {'batch','ctx','fsdp'}, use_global_device_ids=true, to_apply=%region_21.22 | all-reduce | flops 12288 | bytes 98304 | tf_op jit(solution)/shard_map/psum | solution.py:279
  398.0 7.1 %slice.196 = f32[4,512,1024]{2,1,0:T(8,128)} slice(bf16[4,640,1024]{2,1,0:T(8,128)(2,1)} %all-gather.9.cloned.1.call-done), slice={[0:4], [128:640], [0:1024]} | slice | bytes 16777216 | tf_op jit(solution)/shard_map/slice | solution.py:261
  405.1 3.0 slice.194
  408.0 41.2 %all-gather.11.cloned.1.call-done = bf16[8,512,896]{2,1,0:T(8,128)(2,1)} async-done(((bf16[2,512,896]{2,1,0:T(8,128)(2,1)}), bf16[8,512,896]{2,1,0:T(8,128)(2,1)}) %all-gather.11.cloned.1.call-update) | async-done | bytes 7340048 | tf_op jit(solution)/shard_map/all_gather | solution.py:251
  449.2 9.3 %convert_bitcast_fusion = f32[512,2,4,896]{3,0,1,2:T(8,128)} fusion(bf16[4,2,512,896]{3,2,1,0:T(8,128)(2,1)} %bitcast.260), kind=kLoop, calls=%fused_computation | loop fusion | flops 3670016 | bytes 22020096 | tf_op jit(solution)/shard_map/convert_element_type | solution.py:253
  458.5 5.9 %slice.193 = f32[512,2,4,384]{3,0,1,2:T(8,128)} slice(f32[512,2,4,896]{3,0,1,2:T(8,128)} %convert_bitcast_fusion), slice={[0:512], [0:2], [0:4], [0:384]} | slice | bytes 12582912 | tf_op jit(solution)/shard_map/slice | solution.py:254
  464.5 7.8 %slice.195 = f32[512,2,4,512]{3,0,1,2:T(8,128)} slice(f32[512,2,4,896]{3,0,1,2:T(8,128)} %convert_bitcast_fusion), slice={[0:512], [0:2], [0:4], [384:896]} | slice | bytes 16777216 | tf_op jit(solution)/shard_map/slice | solution.py:258
  472.2 6.6 %copy.149 = f32[512,2,4,384]{0,3,2,1:T(8,128)} copy(f32[512,2,4,384]{3,0,1,2:T(8,128)} %slice.193) | data formatting | bytes 12582912 | tf_op jit(solution)/shard_map/slice | solution.py:254
  478.8 6.5 %copy.150 = f32[512,3,2,4,128]{0,4,3,2,1:T(8,128)} copy(f32[512,3,2,4,128]{0,4,1,3,2:T(8,128)} %bitcast.255) | data formatting | bytes 12582912 | tf_op jit(solution)/shard_map/transpose | solution.py:257
  485.3 6.6 %copy.152 = f32[512,3072]{1,0:T(8,128)} copy(f32[512,3072]{0,1:T(8,128)} %bitcast.256) | data formatting | bytes 12582912
  491.9 9.9 %copy.151 = f32[512,2,4,512]{0,3,2,1:T(8,128)} copy(f32[512,2,4,512]{3,0,1,2:T(8,128)} %slice.195) | data formatting | bytes 16777216 | tf_op jit(solution)/shard_map/slice | solution.py:258
  501.8 9.0 %copy.153 = f32[512,4096]{1,0:T(8,128)} copy(f32[512,4096]{0,1:T(8,128)} %bitcast.254) | data formatting | bytes 16777216
  (181 shorter events, 11.8 us)
Async XLA Ops:
  7.2 72.6 %copy-start = (bf16[512,1024]{1,0:T(8,128)(2,1)S(1)}, bf16[512,1024]{1,0:T(8,128)(2,1)}, u32[]{:S(2)}) copy-start(bf16[512,1024]{1,0:T(8,128)(2,1)} %param.20) | copy-start | bytes 3145732
  7.2 60.3 %all-gather.7.cloned.1.call-start = ((), (), s32[]{:S(2)}) async-start(), calls=%async_computation.5 | async-start | bytes 4718592 | tf_op jit(solution)/shard_map/all_gather | solution.py:182
  24.4 7.3 %copy-start.19 = (bf16[1536]{0:T(1024)(128)(2,1)S(1)}, bf16[1536]{0:T(1024)(128)(2,1)}, u32[]{:S(2)}) copy-start(bf16[1536]{0:T(1024)(128)(2,1)} %param.19) | copy-start | bytes 9220
  24.4 7.5 %copy-start.28 = (bf16[512]{0:T(512)(128)(2,1)S(1)}, bf16[512]{0:T(512)(128)(2,1)}, u32[]{:S(2)}) copy-start(bf16[512]{0:T(512)(128)(2,1)} %param.21) | copy-start | bytes 3076
  24.4 7.7 %copy-start.20 = (bf16[2048]{0:T(1024)(128)(2,1)S(1)}, bf16[2048]{0:T(1024)(128)(2,1)}, u32[]{:S(2)}) copy-start(bf16[2048]{0:T(1024)(128)(2,1)} %param.23) | copy-start | bytes 12292
  24.4 7.7 %copy-start.29 = (bf16[512]{0:T(512)(128)(2,1)S(1)}, bf16[512]{0:T(512)(128)(2,1)}, u32[]{:S(2)}) copy-start(bf16[512]{0:T(512)(128)(2,1)} %param.25) | copy-start | bytes 3076
  24.4 8.0 %copy-start.30 = (bf16[512]{0:T(512)(128)(2,1)S(1)}, bf16[512]{0:T(512)(128)(2,1)}, u32[]{:S(2)}) copy-start(bf16[512]{0:T(512)(128)(2,1)} %param.26) | copy-start | bytes 3076
  24.4 8.2 %copy-start.31 = (bf16[512]{0:T(512)(128)(2,1)S(1)}, bf16[512]{0:T(512)(128)(2,1)}, u32[]{:S(2)}) copy-start(bf16[512]{0:T(512)(128)(2,1)} %param.27) | copy-start | bytes 3076
  24.4 8.4 %copy-start.32 = (bf16[512]{0:T(512)(128)(2,1)S(1)}, bf16[512]{0:T(512)(128)(2,1)}, u32[]{:S(2)}) copy-start(bf16[512]{0:T(512)(128)(2,1)} %param.28) | copy-start | bytes 3076
  24.4 8.6 %copy-start.27 = (bf16[512]{0:T(512)(128)(2,1)S(1)}, bf16[512]{0:T(512)(128)(2,1)}, u32[]{:S(2)}) copy-start(bf16[512]{0:T(512)(128)(2,1)} %param.29) | copy-start | bytes 3076
  26.0 41.2 %copy-start.33 = (s32[4]{0:T(128)S(1)}, s32[4]{0:T(128)}, u32[]{:S(2)}) copy-start(s32[4]{0:T(128)} %param.17) | copy-start | bytes 52
  27.4 44.5 %all-to-all-start = ((bf16[2,512,896]{2,1,0:T(8,128)(2,1)}), bf16[2,512,896]{2,1,0:T(8,128)(2,1)S(1)}, u32[]{:S(2)}, u32[]{:S(2)}) async-start(bf16[2,512,896]{2,1,0:T(8,128)(2,1)} %pad_maximum_fusion.1), calls=%async_computation | async-start | bytes 3670016 | tf_op jit(solution)/shard_map/all_to_all | solution.py:170
  66.4 1.0 copy-start.15
  67.1 8.4 %copy-start.21 = (f32[1,4,2,128]{3,1,2,0:T(4,128)}, f32[1,4,2,128]{3,1,2,0:T(4,128)S(1)}, u32[]{:S(2)}) copy-start(f32[1,4,2,128]{3,1,2,0:T(4,128)S(1)} %copy.178) | copy-start | bytes 12292
  67.1 0.5 copy-start.25
  71.9 3.7 copy-start.23
  71.9 3.6 copy-start.9
  75.7 4.0 slice-start
  79.7 1.2 copy-start.8
  79.7 1.2 copy-start.14
  80.6 9.6 %copy-start.17 = (f32[1,4,2,128]{3,2,1,0:T(2,128)S(1)}, f32[1,4,2,128]{3,2,1,0:T(2,128)}, u32[]{:S(2)}) copy-start(f32[1,4,2,128]{3,2,1,0:T(2,128)} %get-tuple-element.119) | copy-start | bytes 12292
  80.6 9.6 %copy-start.16 = (f32[1,4,2,128]{3,2,1,0:T(2,128)S(1)}, f32[1,4,2,128]{3,2,1,0:T(2,128)}, u32[]{:S(2)}) copy-start(f32[1,4,2,128]{3,2,1,0:T(2,128)} %get-tuple-element.118) | copy-start | bytes 12292
  80.6 9.7 %copy-start.34 = (s32[4]{0:T(128)S(1)}, s32[4]{0:T(128)}, u32[]{:S(2)}) copy-start(s32[4]{0:T(128)} %param.17) | copy-start | bytes 52
  80.6 9.7 %copy-start.26 = (f32[8]{0:T(128)S(1)}, f32[8]{0:T(128)}, u32[]{:S(2)}) copy-start(f32[8]{0:T(128)} %copy-done.25) | copy-start | bytes 100
  84.1 30.0 %all-to-all-start.1 = ((bf16[4,2,128,512]{2,1,3,0:T(2,128)(2,1)}), bf16[4,2,128,512]{2,1,3,0:T(2,128)(2,1)S(1)}, u32[]{:S(2)}, u32[]{:S(2)}) async-start(bf16[4,2,128,512]{2,1,3,0:T(2,128)(2,1)} %copy.134), calls=%async_computation.1 | async-start | bytes 2097152 | tf_op jit(solution)/shard_map/all_to_all | solution.py:205
  122.7 1.3 copy-start.6
  123.0 0.8 copy-start.4
  124.0 7.3 %copy-start.24 = (f32[1024]{0:T(1024)S(1)}, f32[1024]{0:T(1024)}, u32[]{:S(2)}) copy-start(f32[1024]{0:T(1024)} %copy-done.23) | copy-start | bytes 12292
  127.6 28.7 %all-to-all-start.2 = ((bf16[4,2,128,512]{2,3,1,0:T(8,128)(2,1)}), bf16[4,2,128,512]{2,3,1,0:T(8,128)(2,1)S(1)}, u32[]{:S(2)}, u32[]{:S(2)}) async-start(bf16[4,2,128,512]{2,3,1,0:T(8,128)(2,1)} %copy.146), calls=%async_computation.2 | async-start | bytes 2097152 | tf_op jit(solution)/shard_map/all_to_all | solution.py:211
  131.1 156.8 %all-reduce.3.cloned.1.call-start = ((), (), s32[]{:S(2)}) async-start(), calls=%async_computation.9 | async-start | bytes 6291456 | tf_op jit(solution)/shard_map/psum | solution.py:248
  131.3 3.7 copy-start.2
  135.0 2.3 copy-start.35
  140.7 1.0 copy-start.37
  141.7 15.9 %copy-start.22 = (f32[1,4,2,128]{3,1,2,0:T(4,128)S(1)}, f32[1,4,2,128]{3,1,2,0:T(4,128)}, u32[]{:S(2)}) copy-start(f32[1,4,2,128]{3,1,2,0:T(4,128)} %copy-done.21) | copy-start | bytes 12292
  157.6 3.2 copy-start.12
  163.4 4.8 copy-start.10
  168.1 184.6 %reduce-scatter.2.cloned.1.call-start = ((), (), s32[]{:S(2)}) async-start(), calls=%async_computation.6 | async-start | bytes 7077888 | tf_op jit(solution)/shard_map/reduce_scatter | solution.py:232
  168.1 2.6 copy-start.11
  170.8 2.0 copy-start.36
  178.4 137.5 %copy-start.3 = (bf16[1,128,1024]{2,1,0:T(8,128)(2,1)S(1)}, bf16[1,128,1024]{2,1,0:T(8,128)(2,1)}, u32[]{:S(2)}) copy-start(bf16[1,128,1024]{2,1,0:T(8,128)(2,1)} %param.15) | copy-start | bytes 786436
  178.4 137.9 %copy-start.5 = (f32[2,512,1,2,64]{1,4,3,0,2:T(8,128)S(1)}, f32[2,512,1,2,64]{1,4,3,0,2:T(8,128)}, u32[]{:S(2)}) copy-start(f32[2,512,1,2,64]{1,4,3,0,2:T(8,128)} %copy-done.4) | copy-start | bytes 1572868
  178.5 137.9 %copy-start.7 = (f32[2,512,1,2,64]{1,4,3,0,2:T(8,128)S(1)}, f32[2,512,1,2,64]{1,4,3,0,2:T(8,128)}, u32[]{:S(2)}) copy-start(f32[2,512,1,2,64]{1,4,3,0,2:T(8,128)} %copy-done.6) | copy-start | bytes 1572868
  178.5 219.5 %all-gather.9.cloned.1.call-start = ((), (), s32[]{:S(2)}) async-start(), calls=%async_computation.7 | async-start | bytes 6553600 | tf_op jit(solution)/shard_map/all_gather | solution.py:252
  287.9 161.3 %all-gather.11.cloned.1.call-start = ((), (), s32[]{:S(2)}) async-start(), calls=%async_computation.8 | async-start | bytes 9175040 | tf_op jit(solution)/shard_map/all_gather | solution.py:251
  315.8 38.7 %copy-start.13 = (bf16[1,128,1024]{2,1,0:T(8,128)(2,1)S(1)}, bf16[1,128,1024]{2,1,0:T(8,128)(2,1)}, u32[]{:S(2)}) copy-start(bf16[1,128,1024]{2,1,0:T(8,128)(2,1)} %param.16) | copy-start | bytes 786436
  396.7 114.1 %copy-start.18 = (f32[512]{0:T(512)}, f32[512]{0:T(512)S(1)}, u32[]{:S(2)}) copy-start(f32[512]{0:T(512)S(1)} %get-tuple-element.159) | copy-start | bytes 6148
  501.8 9.6 %copy-start.1 = (bf16[512,1024]{1,0:T(8,128)(2,1)S(1)}, bf16[512,1024]{1,0:T(8,128)(2,1)}, u32[]{:S(2)}) copy-start(bf16[512,1024]{1,0:T(8,128)(2,1)} %param.20) | copy-start | bytes 3145732
Sparse Core Ops, SparseCore 0:
  10.5 50.6 all-gather.6
  168.2 119.6 all-reduce.2
  291.9 60.7 reduce-scatter.1
  354.2 40.8 all-gather.8
  396.6 52.5 all-gather.10
